TPU v7x, 128 devices: a whole 4x4x4 slice. The times are simulated.
128 devices in a mesh: expert: 4 (over y), feat: 32 (over x, z, core).
Axes of the slice: x: 4, y: 4, z: 4, core: 2. Of those that a mesh axis runs over, the one named last changes fastest.
Arguments:
- tokens: bfloat16 [1024, 4096], P(('expert', 'feat')), may hold values from -6 to 6
- expert_ids: int32 [1024, 2], P(('expert', 'feat')), may hold values from 0 to 7, as said below
- route_weights: bfloat16 [1024, 2], P(('expert', 'feat')), may hold values from 0.099609375 to 1
- gate_proj: bfloat16 [4096, 28672], P(None, ('expert', 'feat')), may hold values from -0.09375 to 0.09375
- up_proj: bfloat16 [4096, 28672], P(None, ('expert', 'feat')), may hold values from -0.09375 to 0.09375
- down_proj: bfloat16 [28672, 4096], P(('expert', 'feat')), may hold values from -0.046875 to 0.046875
- enc_weight: float32 [4096, 32768], P(None, ('expert', 'feat')), may hold values from -0.09375 to 0.09375
- enc_bias: float32 [32768], P(('expert', 'feat')), may hold values from -3 to 3
- log_threshold: float32 [32768], P(('expert', 'feat')), may hold values from -2.3 to 0
- dec_weight: float32 [32768, 4096], P(('expert', 'feat')), may hold values from -0.046875 to 0.046875
Outputs:
- grad_encoder: float32 [4096, 32768], P(None, ('expert', 'feat'))
- grad_decoder: float32 [32768, 4096], P(('expert', 'feat'))
- grad_bias: float32 [32768], P(('expert', 'feat'))
- grad_threshold: float32 [32768], P(('expert', 'feat'))
Inputs may be any that keep to these rules, and one draw needn't show every extreme that they name: `expert_ids`: each token names two different experts of 0 to 7. Among the 8 tokens of one device, each expert below 2 is named by at most 4 tokens; in every draw one of these experts, drawn from the seed and the same for all devices, is named by exactly 4 tokens of every device.
All inputs are finite; a program needn't handle non-finite values.
Results may differ from a plain program's by a relative error of at most 0.0021.
Values may be sent and summed in bfloat16 or wider, within the bound.
A program may use at most 128 MiB of HBM per device.

v0:
```python
import jax
import jax.numpy as jnp
from jax import lax
from jax.sharding import PartitionSpec as P

sharpness = 0.1
kernel_width = 0.5
density_weight = 0.01


def partner(block, axis, stride):
    count = lax.axis_size(axis)
    route = []
    for low in range(count):
        high = low | 1 << stride
        if high != low and high < count:
            route += [(low, high), (high, low)]
    return lax.ppermute(block, axis, route)


def pack_slots(tokens, expert_ids, route_weights, experts):
    capacity = tokens.shape[0] // 2
    window = jnp.arange(experts, dtype=jnp.int32)
    matches = expert_ids[:, :, None] == window[None, None, :]
    named = jnp.sum(matches.astype(jnp.int32), axis=1)
    weighted = jnp.sum(
        jnp.where(matches, route_weights[:, :, None], jnp.zeros((), jnp.bfloat16)), axis=1
    )
    rows = jnp.arange(tokens.shape[0], dtype=jnp.int32)
    earlier = rows[None, :, None] < rows[:, None, None]
    slot_index = jnp.sum(jnp.where(earlier, named[None, :, :], 0), axis=1)
    places = jnp.arange(capacity, dtype=jnp.int32)
    chosen = (named.T[:, None, :] == 1) & (slot_index.T[:, None, :] == places[None, :, None])
    slot_rows = jnp.einsum(
        "ect,td->ecd", chosen.astype(jnp.bfloat16), tokens, preferred_element_type=jnp.float32
    ).astype(jnp.bfloat16)
    slot_weights = jnp.sum(
        jnp.where(chosen, weighted.T[:, None, :], jnp.zeros((), jnp.bfloat16)), axis=2
    )
    return (slot_rows, slot_weights)


def split(value):
    high = lax.reduce_precision(value, 8, 7)
    return (high.astype(jnp.bfloat16), (value - high).astype(jnp.bfloat16))


def product(left, right, dims):
    return lax.dot_general(left, right, (dims, ((), ())), preferred_element_type=jnp.float32)


def body(
    tokens,
    expert_ids,
    route_weights,
    gate_proj,
    up_proj,
    down_proj,
    enc_weight,
    enc_bias,
    log_threshold,
    dec_weight,
):
    copies = 2
    experts = lax.axis_size("expert") // copies
    slot_rows, slot_weights = pack_slots(tokens, expert_ids, route_weights, experts)
    send_rows = jnp.repeat(slot_rows, copies, axis=0)
    send_weights = jnp.repeat(slot_weights, copies, axis=0)
    came_rows, came_weights = (
        lax.all_to_all(send_rows, "expert", split_axis=0, concat_axis=0, tiled=True),
        lax.all_to_all(send_weights, "expert", split_axis=0, concat_axis=0, tiled=True),
    )
    all_rows, all_weights = (
        lax.all_gather(came_rows, "feat", axis=0, tiled=True),
        lax.all_gather(came_weights, "feat", axis=0, tiled=True),
    )
    width = tokens.shape[1]
    token_rows = all_rows.reshape(-1, width)
    row_weights = all_weights.reshape(-1).astype(jnp.float32)
    gate_act = jnp.dot(token_rows, gate_proj, preferred_element_type=jnp.float32)
    up_act = jnp.dot(token_rows, up_proj, preferred_element_type=jnp.float32)
    hidden = (jax.nn.silu(gate_act) * up_act).astype(jnp.bfloat16)
    target_part = jnp.dot(hidden, down_proj, preferred_element_type=jnp.float32)
    rows = ((1,), (0,))
    down = ((0,), (0,))
    enc_high, enc_low = split(enc_weight)
    dec_high, dec_low = split(dec_weight)
    preact = product(token_rows, enc_high, rows) + product(token_rows, enc_low, rows) + enc_bias
    threshold = jnp.exp(log_threshold)
    shifted = preact - threshold
    soft_gate = jax.nn.sigmoid(shifted / sharpness)
    active = preact * soft_gate
    act_high, act_low = split(active)
    recon = product(act_high, dec_high, rows) + product(act_high, dec_low, rows)
    partial_error = recon + product(act_low, dec_high, rows) - target_part
    feat_total = lax.psum_scatter(partial_error, "feat", scatter_dimension=0, tiled=True)
    recon_error = feat_total + partner(feat_total, "expert", 0)
    own_rows = feat_total.shape[0]
    own_weights = lax.dynamic_slice_in_dim(row_weights, lax.axis_index("feat") * own_rows, own_rows)
    own_grad = (2.0 * own_weights[:, None] * recon_error).astype(jnp.bfloat16)
    residual_grad = lax.all_gather(own_grad, "feat", axis=0, tiled=True)
    grad_decoder = product(act_high, residual_grad, down) + product(act_low, residual_grad, down)
    across = ((1,), (1,))
    grad_active = product(residual_grad, dec_high, across) + product(residual_grad, dec_low, across)
    grad_pre = grad_active * soft_gate
    pre_high, pre_low = split(grad_pre)
    grad_encoder = product(token_rows, pre_high, down) + product(token_rows, pre_low, down)
    grad_bias = jnp.sum(grad_pre, axis=0)
    kernel = jnp.maximum(0.0, 1.0 - jnp.abs(shifted) / kernel_width) / kernel_width
    slope_sum = jnp.sum(
        (grad_active * threshold + density_weight * row_weights[:, None]) * kernel, axis=0
    )
    grad_threshold = -threshold * slope_sum
    return (grad_encoder, grad_decoder, grad_bias, grad_threshold)


def solution(mesh):
    in_specs = (
        P(("expert", "feat"), None),
        P(("expert", "feat"), None),
        P(("expert", "feat"), None),
        P(None, ("expert", "feat")),
        P(None, ("expert", "feat")),
        P(("expert", "feat"), None),
        P(None, ("expert", "feat")),
        P(("expert", "feat")),
        P(("expert", "feat")),
        P(("expert", "feat"), None),
    )
    out_specs = (
        P(None, ("expert", "feat")),
        P(("expert", "feat"), None),
        P(("expert", "feat")),
        P(("expert", "feat")),
    )
    return jax.shard_map(body, mesh=mesh, in_specs=in_specs, out_specs=out_specs, check_vma=False)
```

profile of v0, /device:TPU:1, one launch (start us, length us, event | category | flops | bytes accessed | tf_op | source)
XLA Modules:
  0.0 313.5 jit_solution(17543353753348144969)
XLA Ops:
  7.2 0.8 convert_reduce_fusion.1
  8.2 1.0 convolution_convert_fusion
  9.3 9.7 %all_to_all.17 = bf16[4,4,4096]{2,1,0:T(4,128)(2,1)} all-to-all(bf16[4,4,4096]{2,1,0:T(4,128)(2,1)S(1)} %bitcast.22), channel_id=1, replica_groups=mesh['expert'=4,'feat'=32] {'expert'}, dimensions={0} | all-to-all | bytes 262144 | tf_op jit(solution)/shard_map/all_to_all | solution.py:70
  19.1 0.7 exp.10
  19.8 48.0 %all-gather.4.cloned.1.call-done = bf16[128,4,4096]{2,1,0:T(4,128)(2,1)} async-done(((bf16[4,4,4096]{2,1,0:T(4,128)(2,1)}), bf16[128,4,4096]{2,1,0:T(4,128)(2,1)}) %all-gather.4.cloned.1.call-update) | async-done | bytes 4194320 | tf_op jit(solution)/shard_map/all_gather | solution.py:74
  67.8 6.9 %reshape.55 = bf16[512,4096]{1,0:T(8,128)(2,1)} reshape(bf16[128,4,4096]{2,1,0:T(4,128)(2,1)} %all-gather.4.cloned.1.call-done) | data formatting | bytes 8388608 | tf_op jit(solution)/shard_map/reshape | solution.py:78
  74.6 4.9 %fusion.2 = f32[512,256]{1,0:T(8,128)S(1)} fusion(bf16[512,4096]{1,0:T(8,128)(2,1)} %reshape.55, f32[4096,256]{1,0:T(8,128)} %param.16), kind=kOutput, calls=%fused_computation.10 | convolution fusion | flops 1076887552 | bytes 8912896 | tf_op jit(solution)/shard_map/dot_general | solution.py:49
  79.5 1.0 copy-done.7
  80.6 1.3 fusion.6
  81.8 0.9 copy-done.5
  82.8 4.6 %fusion.11 = f32[512,4096]{1,0:T(8,128)} fusion(f32[256,4096]{1,0:T(8,128)S(1)} %copy-done.5, f32[512,256]{1,0:T(8,128)S(1)} %fusion.6, f32[256]{0:T(256)S(1)} %exp.10), kind=kOutput, calls=%fused_computation.23 | convolution fusion | flops 1077936128 | bytes 13108224 | tf_op jit(solution)/shard_map/dot_general | solution.py:49
  87.3 4.5 %fusion.38 = f32[512,4096]{1,0:T(8,128)} fusion(f32[256,4096]{1,0:T(8,128)S(1)} %copy-done.5, f32[512,256]{1,0:T(8,128)S(1)} %fusion.6, f32[256]{0:T(256)S(1)} %exp.10), kind=kOutput, calls=%fused_computation.58 | convolution fusion | flops 1076887552 | bytes 13108224 | tf_op jit(solution)/shard_map/dot_general | solution.py:49
  91.9 1.4 fusion.46
  93.3 8.7 %fusion.8 = f32[512,4096]{1,0:T(8,128)} fusion(bf16[224,4096]{1,0:T(8,128)(2,1)S(1)} %copy-done, bf16[512,4096]{1,0:T(8,128)(2,1)} %reshape.55, bf16[4096,224]{0,1:T(8,128)(2,1)} %param.14, f32[512,224]{0,1:T(8,128)S(1)} %fusion.46), kind=kOutput, calls=%fused_computation.17 | convolution fusion | flops 1879736320 | bytes 16711680 | tf_op jit(solution)/shard_map/dot_general | solution.py:83
  102.0 14.3 %add_subtract_fusion = f32[512,4096]{1,0:T(8,128)} fusion(f32[512,4096]{1,0:T(8,128)} %fusion.8, f32[512,4096]{1,0:T(8,128)} %fusion.38, f32[512,4096]{1,0:T(8,128)} %fusion.11, f32[256,4096]{1,0:T(8,128)} %param.19, f32[512,256]{1,0:T(8,128)S(1)} %fusion.6, f32[256]{0:T(256)S(1)} %exp.10), kind=kOutput, calls=%fused_computation | convolution fusion | flops 1083310080 | bytes 38274048 | tf_op jit(solution)/shard_map/dot_general | solution.py:49
  116.3 0.7 copy-done.10
  117.0 89.5 %reduce-scatter.2.cloned.1.call-done = f32[16,4096]{1,0:T(8,128)} async-done(((f32[512,4096]{1,0:T(8,128)}), f32[16,4096]{1,0:T(8,128)}) %reduce-scatter.2.cloned.1.call-update) | async-done | bytes 262160 | tf_op jit(solution)/shard_map/reduce_scatter | solution.py:96
  206.5 1.2 collective-permute-start
  207.8 0.6 copy.24
  208.4 3.7 %all-to-all-start.1 = ((bf16[4,1,4]{2,1,0:T(2,128)(2,1)}), bf16[4,1,4]{2,1,0:T(2,128)(2,1)S(1)}, u32[]{:S(2)}, u32[]{:S(2)}) async-start(bf16[4,1,4]{2,1,0:T(2,128)(2,1)} %copy.24), calls=%async_computation.1 | async-start | bytes 4096 | tf_op jit(solution)/shard_map/all_to_all | solution.py:71
  212.1 4.1 %all-to-all-done.1 = bf16[4,1,4]{2,1,0:T(2,128)(2,1)S(1)} async-done(((bf16[4,1,4]{2,1,0:T(2,128)(2,1)}), bf16[4,1,4]{2,1,0:T(2,128)(2,1)S(1)}, u32[]{:S(2)}, u32[]{:S(2)}) %all-to-all-start.1) | async-done | bytes 64 | tf_op jit(solution)/shard_map/all_to_all | solution.py:71
  216.2 27.5 %all-gather = bf16[128,1,4]{2,1,0:T(2,128)(2,1)S(1)} all-gather(bf16[4,1,4]{2,1,0:T(2,128)(2,1)S(1)} %all-to-all-done.1), channel_id=2, replica_groups=mesh['expert'=4,'feat'=32] {'feat'}, dimensions={0}, use_global_device_ids=true | all-gather | bytes 1056 | tf_op jit(solution)/shard_map/all_gather | solution.py:75
  244.1 1.7 multiply_convert_fusion
  245.8 43.2 %all-gather.6.cloned.1.call-done = bf16[512,4096]{1,0:T(8,128)(2,1)} async-done(((bf16[16,4096]{1,0:T(8,128)(2,1)}), bf16[512,4096]{1,0:T(8,128)(2,1)}) %all-gather.6.cloned.1.call-update) | async-done | bytes 4194320 | tf_op jit(solution)/shard_map/all_gather | solution.py:101
  289.0 4.9 %fusion.9 = f32[512,256]{1,0:T(8,128)S(1)} fusion(bf16[512,4096]{1,0:T(8,128)(2,1)} %all-gather.6.cloned.1.call-done, f32[256,4096]{1,0:T(8,128)} %param.19), kind=kOutput, calls=%fused_computation.22 | convolution fusion | flops 1076887552 | bytes 8912896 | tf_op jit(solution)/shard_map/dot_general | solution.py:49
  293.9 1.0 copy-done.6
  294.9 2.0 fusion.44
  296.9 0.6 negate_multiply_fusion
  297.5 1.3 fusion.23
  298.8 3.3 %convolution_add_fusion.1 = f32[4096,256]{1,0:T(8,128)} fusion(f32[4096,256]{1,0:T(8,128)S(1)} %fusion.23, bf16[512,4096]{1,0:T(8,128)(2,1)S(1)} %copy-done.3, f32[512,256]{1,0:T(8,128)S(1)} %get-tuple-element.5), kind=kOutput, calls=%fused_computation.6 | convolution fusion | flops 1075183616 | bytes 13107200 | tf_op jit(solution)/shard_map/dot_general | solution.py:49
  302.1 1.4 fusion.25
  303.5 3.5 %convolution_add_fusion = f32[256,4096]{1,0:T(8,128)} fusion(f32[256,4096]{1,0:T(8,128)S(1)} %fusion.25, bf16[512,4096]{1,0:T(8,128)(2,1)S(1)} %copy-done.4, f32[512,256]{1,0:T(8,128)S(1)} %fusion.6, f32[256]{0:T(256)S(1)} %exp.10), kind=kOutput, calls=%fused_computation.5 | convolution fusion | flops 1075838976 | bytes 13108224 | tf_op jit(solution)/shard_map/dot_general | solution.py:49
  (40 shorter events, 0.9 us)
Async XLA Ops:
  7.2 86.1 %copy-start = (bf16[224,4096]{1,0:T(8,128)(2,1)S(1)}, bf16[224,4096]{1,0:T(8,128)(2,1)}, u32[]{:S(2)}) copy-start(bf16[224,4096]{1,0:T(8,128)(2,1)} %param.15) | copy-start | bytes 5505028
  7.2 60.6 %all-gather.4.cloned.1.call-start = ((), (), s32[]{:S(2)}) async-start(), calls=%async_computation.3 | async-start | bytes 4325376 | tf_op jit(solution)/shard_map/all_gather | solution.py:74
  19.0 187.5 %reduce-scatter.2.cloned.1.call-start = ((), (), s32[]{:S(2)}) async-start(), calls=%async_computation.4 | async-start | bytes 8650752 | tf_op jit(solution)/shard_map/reduce_scatter | solution.py:96
  74.6 4.9 %copy-start.2 = (bf16[512,4096]{1,0:T(8,128)(2,1)S(1)}, bf16[512,4096]{1,0:T(8,128)(2,1)}, u32[]{:S(2)}) copy-start(bf16[512,4096]{1,0:T(8,128)(2,1)} %reshape.55) | copy-start | bytes 12582916
  74.6 5.9 %copy-start.7 = (f32[4096,256]{1,0:T(8,128)S(1)}, f32[4096,256]{1,0:T(8,128)}, u32[]{:S(2)}) copy-start(f32[4096,256]{1,0:T(8,128)} %param.16) | copy-start | bytes 12582916
  74.6 5.9 %copy-start.8 = (f32[256]{0:T(256)S(1)}, f32[256]{0:T(256)}, u32[]{:S(2)}) copy-start(f32[256]{0:T(256)} %param.17) | copy-start | bytes 3076
  80.6 2.2 copy-start.5
  87.3 4.5 %copy-start.12 = (bf16[4096,224]{0,1:T(8,128)(2,1)S(1)}, bf16[4096,224]{0,1:T(8,128)(2,1)}, u32[]{:S(2)}) copy-start(bf16[4096,224]{0,1:T(8,128)(2,1)} %param.13) | copy-start | bytes 5505028
  116.3 0.7 copy-start.10
  116.3 0.7 copy-start.11
  206.5 37.6 %collective-permute-start = (f32[16,4096]{1,0:T(8,128)}, f32[16,4096]{1,0:T(8,128)S(1)}, u32[]{:S(2)}, u32[]{:S(2)}) collective-permute-start(f32[16,4096]{1,0:T(8,128)} %reduce-scatter.2.cloned.1.call-done), channel_id=1, source_target_pairs={{0,32},{32,0},{64,96},{96,64},{1,33},{33,1},{65,97},{97,65},{2,34}... | collective-permute-start | bytes 786440 | tf_op jit(solution)/shard_map/ppermute | solution.py:18
  208.4 7.8 %all-to-all-start.1 = ((bf16[4,1,4]{2,1,0:T(2,128)(2,1)}), bf16[4,1,4]{2,1,0:T(2,128)(2,1)S(1)}, u32[]{:S(2)}, u32[]{:S(2)}) async-start(bf16[4,1,4]{2,1,0:T(2,128)(2,1)} %copy.24), calls=%async_computation.1 | async-start | bytes 4096 | tf_op jit(solution)/shard_map/all_to_all | solution.py:71
  212.1 76.9 %all-gather.6.cloned.1.call-start = ((), (), s32[]{:S(2)}) async-start(), calls=%async_computation.5 | async-start | bytes 4325376 | tf_op jit(solution)/shard_map/all_gather | solution.py:101
  289.0 4.9 %copy-start.4 = (bf16[512,4096]{1,0:T(8,128)(2,1)S(1)}, bf16[512,4096]{1,0:T(8,128)(2,1)}, u32[]{:S(2)}) copy-start(bf16[512,4096]{1,0:T(8,128)(2,1)} %all-gather.6.cloned.1.call-done) | copy-start | bytes 12582916
  289.0 5.9 %copy-start.6 = (f32[256,4096]{1,0:T(8,128)S(1)}, f32[256,4096]{1,0:T(8,128)}, u32[]{:S(2)}) copy-start(f32[256,4096]{1,0:T(8,128)} %param.19) | copy-start | bytes 12582916
  294.9 2.0 copy-start.9
  294.9 2.6 copy-start.3
  302.1 4.9 %copy-start.1 = (bf16[224,4096]{1,0:T(8,128)(2,1)S(1)}, bf16[224,4096]{1,0:T(8,128)(2,1)}, u32[]{:S(2)}) copy-start(bf16[224,4096]{1,0:T(8,128)(2,1)} %param.15) | copy-start | bytes 5505028
Sparse Core Ops, SparseCore 0:
  19.1 48.5 all-gather.3
  116.5 89.9 reduce-scatter.1
  245.9 43.0 all-gather.5
where the time goes:
time: 314 us
  waiting for transfers between devices  185 us (59%)
  matrix products  57.1 us (18%)
  blocking collectives  37.3 us (12%)
  between operations  13.9 us (4%)
  local copies, waits for them, and re-layouts  11.9 us (4%)
  starting transfers between devices  4.98 us (2%)
  other arithmetic  3.61 us (1%)
    reduce_scatter x1, waiting for transfers between devices, body(): lax.psum_scatter(partial_error, 'feat', scatter_dimension=0, tiled=True)  89.5 us
    all_gather x1, waiting for transfers between devices, body(): lax.all_gather(came_rows, 'feat', axis=0, tiled=True)  48 us
    dot_general x11, matrix products, product(): lax.dot_general(left, right, (dims, ((), ())), preferred_element_type=jnp...  45.9 us
    all_gather x1, waiting for transfers between devices, body(): residual_grad = lax.all_gather(own_grad, 'feat', axis=0, tiled=True)  43.2 us
    all_gather x1, blocking collectives, body(): lax.all_gather(came_weights, 'feat', axis=0, tiled=True)  27.5 us
    all_to_all x1, blocking collectives, body(): lax.all_to_all(send_rows, 'expert', split_axis=0, concat_axis=0, tiled=True)  9.75 us
    dot_general x1, matrix products, body(): target_part = jnp.dot(hidden, down_proj, preferred_element_type=jnp.float32)  8.72 us
    reshape x1, local copies, waits for them, and re-layouts, body(): token_rows = all_rows.reshape(-1, width)  6.87 us
  transfers between devices with their start and end apart: 5, of which 4 were waited for; matrix products, arithmetic and copies ran while one was open for 1% of the time, Pallas kernels for 0%

commit v1 on v0

--- a/solution.py
+++ b/solution.py
@@ -6,6 +6,13 @@
 sharpness = 0.1
 kernel_width = 0.5
 density_weight = 0.01
+
+
+def gather_over(x, axis, dim):
+    n_dev = lax.axis_size(axis)
+    parts = jnp.stack([x for _ in range(n_dev)])
+    parts = lax.all_to_all(parts, axis, split_axis=0, concat_axis=0)
+    return jnp.concatenate(parts, axis=dim)
 
 
 def partner(block, axis, stride):
@@ -72,7 +79,7 @@
     )
     all_rows, all_weights = (
         lax.all_gather(came_rows, "feat", axis=0, tiled=True),
-        lax.all_gather(came_weights, "feat", axis=0, tiled=True),
+        gather_over(came_weights, "feat", 0),
     )
     width = tokens.shape[1]
     token_rows = all_rows.reshape(-1, width)

time: 314 us -> 302 us (0.962)
  blocking collectives: 37.3 us -> 17.4 us
  starting transfers between devices: 4.98 us -> 10.5 us
    all_gather x1 -> x0, blocking collectives: 27.5 us -> none  [body(): lax.all_gather(came_weights, 'feat', axis=0, tiled=True)]
    all_to_all x0 -> x1, blocking collectives: none -> 7.67 us  [body(): lax.all_to_all(send_weights, 'expert', split_axis=0, concat_axis=0, tiled...]
    all_to_all x1, starting transfers between devices: 3.71 us -> 8.95 us  [gather_over(): parts = lax.all_to_all(parts, axis, split_axis=0, concat_axis=0)]
where the time goes in v1:
time: 302 us; the launch traced here: 301 us
  waiting for transfers between devices  188 us (62%)
  matrix products  57.1 us (19%)
  blocking collectives  17.4 us (6%)
  between operations  13.9 us (5%)
  local copies, waits for them, and re-layouts  11.3 us (4%)
  starting transfers between devices  10.5 us (3%)
  other arithmetic  3.42 us (1%)
    reduce_scatter x1, waiting for transfers between devices, body(): lax.psum_scatter(partial_error, 'feat', scatter_dimension=0, tiled=True)  90.1 us
    all_gather x1, waiting for transfers between devices, body(): lax.all_gather(came_rows, 'feat', axis=0, tiled=True)  48 us
    dot_general x11, matrix products, product(): lax.dot_general(left, right, (dims, ((), ())), preferred_element_type=jnp...  45.9 us
    all_gather x1, waiting for transfers between devices, body(): residual_grad = lax.all_gather(own_grad, 'feat', axis=0, tiled=True)  42.4 us
    all_to_all x1, blocking collectives, body(): lax.all_to_all(send_rows, 'expert', split_axis=0, concat_axis=0, tiled=True)  9.75 us
    all_to_all x1, starting transfers between devices, gather_over(): parts = lax.all_to_all(parts, axis, split_axis=0, concat_axis=0)  8.95 us
    dot_general x1, matrix products, body(): target_part = jnp.dot(hidden, down_proj, preferred_element_type=jnp.float32)  8.71 us
    all_to_all x1, blocking collectives, body(): lax.all_to_all(send_weights, 'expert', split_axis=0, concat_axis=0, tiled...  7.67 us
  transfers between devices with their start and end apart: 5, of which 4 were waited for; matrix products, arithmetic and copies ran while one was open for 1% of the time, Pallas kernels for 0%

profile of v1, /device:TPU:1, one launch (start us, length us, event | category | flops | bytes accessed | tf_op | source)
XLA Modules:
  0.0 301.2 jit_solution(10796201367737204666)
XLA Ops:
  7.2 0.8 convert_reduce_fusion
  8.2 1.0 convolution_convert_fusion
  9.3 9.7 %all_to_all.19 = bf16[4,4,4096]{2,1,0:T(4,128)(2,1)} all-to-all(bf16[4,4,4096]{2,1,0:T(4,128)(2,1)S(1)} %bitcast.25), channel_id=1, replica_groups=mesh['expert'=4,'feat'=32] {'expert'}, dimensions={0} | all-to-all | bytes 262144 | tf_op jit(solution)/shard_map/all_to_all | solution.py:77
  19.1 0.7 exp.10
  19.8 48.0 %all-gather.3.cloned.1.call-done = bf16[128,4,4096]{2,1,0:T(4,128)(2,1)} async-done(((bf16[4,4,4096]{2,1,0:T(4,128)(2,1)}), bf16[128,4,4096]{2,1,0:T(4,128)(2,1)}) %all-gather.3.cloned.1.call-update) | async-done | bytes 4194320 | tf_op jit(solution)/shard_map/all_gather | solution.py:81
  67.8 6.9 %reshape.57 = bf16[512,4096]{1,0:T(8,128)(2,1)} reshape(bf16[128,4,4096]{2,1,0:T(4,128)(2,1)} %all-gather.3.cloned.1.call-done) | data formatting | bytes 8388608 | tf_op jit(solution)/shard_map/reshape | solution.py:85
  74.6 4.9 %fusion.2 = f32[512,256]{1,0:T(8,128)S(1)} fusion(bf16[512,4096]{1,0:T(8,128)(2,1)} %reshape.57, f32[4096,256]{1,0:T(8,128)} %param.16), kind=kOutput, calls=%fused_computation.10 | convolution fusion | flops 1076887552 | bytes 8912896 | tf_op jit(solution)/shard_map/dot_general | solution.py:56
  79.5 1.0 copy-done.7
  80.6 1.3 fusion.6
  81.8 0.9 copy-done.5
  82.8 4.6 %fusion.11 = f32[512,4096]{1,0:T(8,128)} fusion(f32[256,4096]{1,0:T(8,128)S(1)} %copy-done.5, f32[512,256]{1,0:T(8,128)S(1)} %fusion.6, f32[256]{0:T(256)S(1)} %exp.10), kind=kOutput, calls=%fused_computation.23 | convolution fusion | flops 1077936128 | bytes 13108224 | tf_op jit(solution)/shard_map/dot_general | solution.py:56
  87.3 4.5 %fusion.38 = f32[512,4096]{1,0:T(8,128)} fusion(f32[256,4096]{1,0:T(8,128)S(1)} %copy-done.5, f32[512,256]{1,0:T(8,128)S(1)} %fusion.6, f32[256]{0:T(256)S(1)} %exp.10), kind=kOutput, calls=%fused_computation.58 | convolution fusion | flops 1076887552 | bytes 13108224 | tf_op jit(solution)/shard_map/dot_general | solution.py:56
  91.8 1.4 fusion.46
  93.3 8.7 %fusion.8 = f32[512,4096]{1,0:T(8,128)} fusion(bf16[224,4096]{1,0:T(8,128)(2,1)S(1)} %copy-done, bf16[512,4096]{1,0:T(8,128)(2,1)} %reshape.57, bf16[4096,224]{0,1:T(8,128)(2,1)} %param.14, f32[512,224]{0,1:T(8,128)S(1)} %fusion.46), kind=kOutput, calls=%fused_computation.17 | convolution fusion | flops 1879736320 | bytes 16711680 | tf_op jit(solution)/shard_map/dot_general | solution.py:90
  102.0 14.3 %add_subtract_fusion = f32[512,4096]{1,0:T(8,128)} fusion(f32[512,4096]{1,0:T(8,128)} %fusion.8, f32[512,4096]{1,0:T(8,128)} %fusion.38, f32[512,4096]{1,0:T(8,128)} %fusion.11, f32[256,4096]{1,0:T(8,128)} %param.19, f32[512,256]{1,0:T(8,128)S(1)} %fusion.6, f32[256]{0:T(256)S(1)} %exp.10), kind=kOutput, calls=%fused_computation | convolution fusion | flops 1083310080 | bytes 38274048 | tf_op jit(solution)/shard_map/dot_general | solution.py:56
  116.3 90.1 %reduce-scatter.2.cloned.1.call-done = f32[16,4096]{1,0:T(8,128)} async-done(((f32[512,4096]{1,0:T(8,128)}), f32[16,4096]{1,0:T(8,128)}) %reduce-scatter.2.cloned.1.call-update) | async-done | bytes 262160 | tf_op jit(solution)/shard_map/reduce_scatter | solution.py:103
  206.5 1.2 collective-permute-start
  207.8 7.7 %all_to_all.20 = bf16[4,1,4]{2,1,0:T(2,128)(2,1)S(1)} all-to-all(bf16[4,1,4]{2,1,0:T(2,128)(2,1)S(1)} %copy.28), channel_id=1, replica_groups=mesh['expert'=4,'feat'=32] {'expert'}, dimensions={0} | all-to-all | bytes 64 | tf_op jit(solution)/shard_map/all_to_all | solution.py:78
  215.5 0.6 stack.5
  216.1 9.0 %all-to-all-start.2 = ((bf16[32,4,4]{2,1,0:T(4,128)(2,1)}), bf16[32,4,4]{2,1,0:T(4,128)(2,1)S(1)}, u32[]{:S(2)}, u32[]{:S(2)}) async-start(bf16[32,4,4]{2,1,0:T(4,128)(2,1)} %stack.5), calls=%async_computation.2 | async-start | bytes 65536 | tf_op jit(solution)/shard_map/all_to_all | solution.py:14
  225.1 0.2 all-gather.5.cloned.1.call-start
  225.3 7.0 %all-to-all-done.2 = bf16[32,4,4]{2,1,0:T(4,128)(2,1)S(1)} async-done(((bf16[32,4,4]{2,1,0:T(4,128)(2,1)}), bf16[32,4,4]{2,1,0:T(4,128)(2,1)S(1)}, u32[]{:S(2)}, u32[]{:S(2)}) %all-to-all-start.2) | async-done | bytes 1056 | tf_op jit(solution)/shard_map/all_to_all | solution.py:14
  232.6 1.7 multiply_convert_fusion
  234.3 42.4 %all-gather.5.cloned.1.call-done = bf16[512,4096]{1,0:T(8,128)(2,1)} async-done(((bf16[16,4096]{1,0:T(8,128)(2,1)}), bf16[512,4096]{1,0:T(8,128)(2,1)}) %all-gather.5.cloned.1.call-update) | async-done | bytes 4194320 | tf_op jit(solution)/shard_map/all_gather | solution.py:108
  276.7 4.9 %fusion.9 = f32[512,256]{1,0:T(8,128)S(1)} fusion(bf16[512,4096]{1,0:T(8,128)(2,1)} %all-gather.5.cloned.1.call-done, f32[256,4096]{1,0:T(8,128)} %param.19), kind=kOutput, calls=%fused_computation.22 | convolution fusion | flops 1076887552 | bytes 8912896 | tf_op jit(solution)/shard_map/dot_general | solution.py:56
  281.6 1.0 copy-done.6
  282.6 2.0 fusion.44
  284.6 0.6 negate_multiply_fusion
  285.2 1.3 fusion.23
  286.5 3.3 %convolution_add_fusion.1 = f32[4096,256]{1,0:T(8,128)} fusion(f32[4096,256]{1,0:T(8,128)S(1)} %fusion.23, bf16[512,4096]{1,0:T(8,128)(2,1)S(1)} %copy-done.3, f32[512,256]{1,0:T(8,128)S(1)} %get-tuple-element.5), kind=kOutput, calls=%fused_computation.6 | convolution fusion | flops 1075183616 | bytes 13107200 | tf_op jit(solution)/shard_map/dot_general | solution.py:56
  289.8 1.4 fusion.25
  291.2 3.5 %convolution_add_fusion = f32[256,4096]{1,0:T(8,128)} fusion(f32[256,4096]{1,0:T(8,128)S(1)} %fusion.25, bf16[512,4096]{1,0:T(8,128)(2,1)S(1)} %copy-done.4, f32[512,256]{1,0:T(8,128)S(1)} %fusion.6, f32[256]{0:T(256)S(1)} %exp.10), kind=kOutput, calls=%fused_computation.5 | convolution fusion | flops 1075838976 | bytes 13108224 | tf_op jit(solution)/shard_map/dot_general | solution.py:56
  (41 shorter events, 0.7 us)
Async XLA Ops:
  7.2 86.1 %copy-start = (bf16[224,4096]{1,0:T(8,128)(2,1)S(1)}, bf16[224,4096]{1,0:T(8,128)(2,1)}, u32[]{:S(2)}) copy-start(bf16[224,4096]{1,0:T(8,128)(2,1)} %param.15) | copy-start | bytes 5505028
  7.2 60.6 %all-gather.3.cloned.1.call-start = ((), (), s32[]{:S(2)}) async-start(), calls=%async_computation.4 | async-start | bytes 4325376 | tf_op jit(solution)/shard_map/all_gather | solution.py:81
  19.0 187.5 %reduce-scatter.2.cloned.1.call-start = ((), (), s32[]{:S(2)}) async-start(), calls=%async_computation.5 | async-start | bytes 8650752 | tf_op jit(solution)/shard_map/reduce_scatter | solution.py:103
  74.6 4.9 %copy-start.2 = (bf16[512,4096]{1,0:T(8,128)(2,1)S(1)}, bf16[512,4096]{1,0:T(8,128)(2,1)}, u32[]{:S(2)}) copy-start(bf16[512,4096]{1,0:T(8,128)(2,1)} %reshape.57) | copy-start | bytes 12582916
  74.6 5.9 %copy-start.7 = (f32[4096,256]{1,0:T(8,128)S(1)}, f32[4096,256]{1,0:T(8,128)}, u32[]{:S(2)}) copy-start(f32[4096,256]{1,0:T(8,128)} %param.16) | copy-start | bytes 12582916
  74.6 5.9 %copy-start.8 = (f32[256]{0:T(256)S(1)}, f32[256]{0:T(256)}, u32[]{:S(2)}) copy-start(f32[256]{0:T(256)} %param.17) | copy-start | bytes 3076
  80.6 2.2 copy-start.5
  87.3 4.5 %copy-start.12 = (bf16[4096,224]{0,1:T(8,128)(2,1)S(1)}, bf16[4096,224]{0,1:T(8,128)(2,1)}, u32[]{:S(2)}) copy-start(bf16[4096,224]{0,1:T(8,128)(2,1)} %param.13) | copy-start | bytes 5505028
  116.3 91.4 %copy-start.10 = (s32[8,2]{0,1:T(2,128)S(1)}, s32[8,2]{0,1:T(2,128)}, u32[]{:S(2)}) copy-start(s32[8,2]{0,1:T(2,128)} %param.11) | copy-start | bytes 196
  116.3 91.4 %copy-start.11 = (bf16[8,2]{0,1:T(2,128)(2,1)S(1)}, bf16[8,2]{0,1:T(2,128)(2,1)}, u32[]{:S(2)}) copy-start(bf16[8,2]{0,1:T(2,128)(2,1)} %param.12) | copy-start | bytes 100
  206.5 26.1 %collective-permute-start = (f32[16,4096]{1,0:T(8,128)}, f32[16,4096]{1,0:T(8,128)S(1)}, u32[]{:S(2)}, u32[]{:S(2)}) collective-permute-start(f32[16,4096]{1,0:T(8,128)} %reduce-scatter.2.cloned.1.call-done), channel_id=1, source_target_pairs={{0,32},{32,0},{64,96},{96,64},{1,33},{33,1},{65,97},{97,65},{2,34}... | collective-permute-start | bytes 786440 | tf_op jit(solution)/shard_map/ppermute | solution.py:25
  216.1 16.2 %all-to-all-start.2 = ((bf16[32,4,4]{2,1,0:T(4,128)(2,1)}), bf16[32,4,4]{2,1,0:T(4,128)(2,1)S(1)}, u32[]{:S(2)}, u32[]{:S(2)}) async-start(bf16[32,4,4]{2,1,0:T(4,128)(2,1)} %stack.5), calls=%async_computation.2 | async-start | bytes 65536 | tf_op jit(solution)/shard_map/all_to_all | solution.py:14
  225.1 51.6 %all-gather.5.cloned.1.call-start = ((), (), s32[]{:S(2)}) async-start(), calls=%async_computation.6 | async-start | bytes 4325376 | tf_op jit(solution)/shard_map/all_gather | solution.py:108
  276.7 4.9 %copy-start.4 = (bf16[512,4096]{1,0:T(8,128)(2,1)S(1)}, bf16[512,4096]{1,0:T(8,128)(2,1)}, u32[]{:S(2)}) copy-start(bf16[512,4096]{1,0:T(8,128)(2,1)} %all-gather.5.cloned.1.call-done) | copy-start | bytes 12582916
  276.7 5.9 %copy-start.6 = (f32[256,4096]{1,0:T(8,128)S(1)}, f32[256,4096]{1,0:T(8,128)}, u32[]{:S(2)}) copy-start(f32[256,4096]{1,0:T(8,128)} %param.19) | copy-start | bytes 12582916
  282.6 2.0 copy-start.9
  282.6 2.6 copy-start.3
  289.8 4.9 %copy-start.1 = (bf16[224,4096]{1,0:T(8,128)(2,1)S(1)}, bf16[224,4096]{1,0:T(8,128)(2,1)}, u32[]{:S(2)}) copy-start(bf16[224,4096]{1,0:T(8,128)(2,1)} %param.15) | copy-start | bytes 5505028
Sparse Core Ops, SparseCore 0:
  19.1 48.5 all-gather.2
  116.5 89.9 reduce-scatter.1
  234.4 42.2 all-gather.4
